TPU v7x, 512 devices: a whole 4x4x16 slice. The times are simulated.
512 devices in a mesh: space: 32 (over z, core), mode: 16 (over y, x).
Axes of the slice: x: 4, y: 4, z: 16, core: 2. Of those that a mesh axis runs over, the one named last changes fastest.
Arguments:
- basis: float32 [3, 256, 16, 8, 2048], P(None, 'space', None, None, 'mode'), may hold values from -132 to 132
- mean_flow: float32 [3, 256, 16, 8], P(None, 'space'), may hold values from -3 to 3
- flow_gradient: float32 [3, 3, 256, 16, 8], P(None, None, 'space'), may hold values from -2 to 2
- viscosity: float32 [256, 16, 8], P('space'), may hold values from 0.02 to 0.2
Outputs:
- reduced: float32 [2048, 2048], P('mode', 'space')
- advected: float32 [3, 256, 16, 8, 2048], P(None, 'space', None, None, 'mode')
- r_factor: float32 [2048, 128], P('mode')
All inputs are finite; a program needn't handle non-finite values.
Results may differ from a plain program's by a relative error of at most 0.00074.
Values may be sent and summed in bfloat16 or wider, within the bound.
No kernel may reach another device: no remote copies, remote signals or barrier semaphores. Data moves between devices by JAX's collectives and lax.ppermute only.
A program may use at most 64 MiB of HBM per device.

v0:
```python
import jax
import jax.numpy as jnp
from jax import lax
from jax.sharding import PartitionSpec as P


def extended(cells, sides, width):
    for axis, dim in sides:
        count = lax.axis_size(axis)
        ends = count - 1
        head = lax.slice_in_dim(cells, 0, width, axis=dim)
        tail = lax.slice_in_dim(cells, cells.shape[dim] - width, cells.shape[dim], axis=dim)
        cells = jnp.concatenate(
            [
                lax.ppermute(tail, axis, [(i, (i + 1) % count) for i in range(ends)]),
                cells,
                lax.ppermute(head, axis, [((i + 1) % count, i) for i in range(ends)]),
            ],
            axis=dim,
        )
    return cells


def transport(padded, mean_flow, flow_gradient, viscosity):
    center = padded[:, 1:-1]
    widen_y = jnp.pad(center, ((0, 0), (0, 0), (1, 1), (0, 0), (0, 0)))
    widen_z = jnp.pad(center, ((0, 0), (0, 0), (0, 0), (1, 1), (0, 0)))
    east_side = padded[:, 2:]
    west_side = padded[:, :-2]
    north_side = widen_y[:, :, 2:]
    south_side = widen_y[:, :, :-2]
    upper_side = widen_z[:, :, :, 2:]
    lower_side = widen_z[:, :, :, :-2]
    laplacian = (
        east_side + west_side + north_side + south_side + upper_side + lower_side - 6.0 * center
    )
    advection = 0.5 * (
        mean_flow[0][None, :, :, :, None] * (east_side - west_side)
        + mean_flow[1][None, :, :, :, None] * (north_side - south_side)
        + mean_flow[2][None, :, :, :, None] * (upper_side - lower_side)
    )
    coupling = flow_gradient[:, 0][..., None] * center[0][None]
    coupling = coupling + flow_gradient[:, 1][..., None] * center[1][None]
    coupling = coupling + flow_gradient[:, 2][..., None] * center[2][None]
    return viscosity[None, :, :, :, None] * laplacian - advection - coupling


def apply_inverse(field, lower_factor):
    width = field.shape[4]
    flat_rows = field.reshape(-1, width)
    solved = jax.scipy.linalg.solve_triangular(lower_factor, flat_rows.T, lower=True)
    return solved.T.reshape(field.shape)


def body(basis, mean_flow, flow_gradient, viscosity):
    cells_x = basis.shape[1]
    cells_y = basis.shape[2]
    cells_z = basis.shape[3]
    panel_width = basis.shape[4]
    weight = 1.0 / (3 * cells_x * cells_y * cells_z * lax.axis_size("space"))
    flat_basis = basis.reshape(-1, panel_width)
    gram_local = (
        jnp.dot(
            flat_basis.T,
            flat_basis,
            precision=lax.Precision.HIGHEST,
            preferred_element_type=jnp.float32,
        )
        * weight
    )
    gram = lax.psum(gram_local, "space")
    lower_factor = jnp.linalg.cholesky(gram)
    ortho = apply_inverse(basis, lower_factor)
    padded_ortho = extended(ortho, (("space", 1),), 1)
    advected = transport(padded_ortho, mean_flow, flow_gradient, viscosity)
    rounded_images = advected.astype(jnp.bfloat16)
    rounded_rows = ortho.astype(jnp.bfloat16).reshape(-1, panel_width)
    panel_piece = lax.all_gather(rounded_images, "mode", axis=4, tiled=True)
    piece_rows = panel_piece.reshape(-1, panel_piece.shape[4])
    strip = (
        jnp.einsum("ra,rk->ak", rounded_rows, piece_rows, preferred_element_type=jnp.float32)
        * weight
    )
    reduced = lax.psum_scatter(strip, "space", scatter_dimension=1, tiled=True)
    return (reduced, advected, lower_factor.T)


def solution(mesh):
    placed = (
        P(None, "space", None, None, "mode"),
        P(None, "space", None, None),
        P(None, None, "space", None, None),
        P("space", None, None),
    )
    return jax.shard_map(
        body,
        mesh=mesh,
        in_specs=placed,
        out_specs=(P("mode", "space"), P(None, "space", None, None, "mode"), P("mode", None)),
        check_vma=False,
    )
```

profile of v0, /device:TPU:2, one launch (start us, length us, event | category | flops | bytes accessed | tf_op | source)
XLA Modules:
  0.0 491.2 jit_solution(15039007794072252386)
XLA Ops:
  7.2 0.0 copy-start
  7.2 0.0 copy-start.5
  7.2 0.0 copy-start.6
  7.2 0.0 all-reduce.4.cloned.1.call-start
  7.2 1.3 copy-done
  8.6 3.3 fusion.8
  11.8 0.0 all-reduce.4.cloned.1.call-update
  11.9 0.0 all-gather.2.cloned.1.call-start
  11.9 0.0 copy-done.5
  12.0 0.0 copy-done.6
  12.0 0.6 slice_bitcast_fusion.5
  12.6 186.8 %all-reduce.4.cloned.1.call-done = f32[128,128]{0,1:T(8,128)} async-done(((f32[128,128]{0,1:T(8,128)}), f32[128,128]{0,1:T(8,128)}) %all-reduce.4.cloned.1.call-update) | async-done | bytes 65552 | tf_op jit(solution)/shard_map/psum | solution.py:71
  199.4 0.9 copy.27
  200.3 0.9 fusion.11
  201.2 11.7 %cholesky.16 = f32[128,128]{1,0:T(8,128)S(1)} custom-call(f32[128,128]{1,0:T(8,128)S(1)} %fusion.11), custom_call_target="Cholesky" | custom-call | tf_op jit(solution)/shard_map/jit(cholesky)/cholesky | solution.py:72
  212.9 0.6 compare_reduce_fusion
  213.5 0.7 fusion.12
  214.2 10.4 %custom-call.7 = f32[1,128,128]{1,2,0:T(8,128)} custom-call(f32[1,128,128]{2,1,0:T(8,128)S(1)} %get-tuple-element.23), custom_call_target="InvertDiagBlocksLowerTriangular" | custom-call | tf_op jit(solution)/shard_map/jit(_solve_triangular)/triangular_solve | solution.py:51
  224.7 2.3 convolution_bitcast_fusion
  227.0 1.6 copy.28
  228.6 1.7 copy.30
  230.3 0.0 copy-start.1
  230.3 0.8 fusion.14
  231.1 1.3 collective-permute-start
  232.4 3.7 collective-permute-start.1
  236.1 1.2 fusion.15
  237.3 0.0 copy-done.1
  237.3 0.0 copy-start.4
  237.3 1.3 copy.36
  238.6 0.9 copy.37
  239.5 0.0 copy-done.4
  239.5 1.0 copy.40
  240.5 0.0 copy-start.2
  240.5 2.1 copy.41
  242.6 2.1 copy.38
  244.7 1.1 copy.39
  245.8 0.0 collective-permute-done
  245.8 0.0 collective-permute-done.1
  245.8 0.0 copy-done.2
  245.8 4.9 %fusion.13 = (bf16[3,8,16,8,128]{4,2,3,1,0:T(8,128)(2,1)}, f32[3,8,16,8,128]{4,2,3,1,0:T(8,128)}) fusion(f32[8,16,8,128]{3,1,2,0:T(8,128)} %copy.41, f32[3,8,16,8]{2,3,1,0:T(8,128)S(1)} %get-tuple-element.17, f32[8,16,8,128]{3,1,2,0:T(8,128)S(1)} %copy.39, f32[3,8,16,8]{2,3,1,0:T(8,128)S(1)} %get-tuple-element.18, f32[8,16,8,128]{3,1,2,0:T(8,128)} %copy.37, ...), kind=kLoop, calls=%fused_computation.31 | loop fusion | flops 10616832 | bytes 5951488 | tf_op jit(solution)/shard_map/convert_element_type | solution.py:76
  250.8 0.0 all-gather.2.cloned.1.call-update
  250.8 0.0 reduce-scatter.2.cloned.1.call-start
  250.9 110.3 %all-gather.2.cloned.1.call-done = bf16[3,8,16,8,2048]{4,2,3,1,0:T(8,128)(2,1)} async-done(((bf16[3,8,16,8,128]{4,2,3,1,0:T(8,128)(2,1)}), bf16[3,8,16,8,2048]{4,2,3,1,0:T(8,128)(2,1)}) %all-gather.2.cloned.1.call-update) | async-done | bytes 12582928 | tf_op jit(solution)/shard_map/all_gather | solution.py:78
  361.1 0.0 copy-start.3
  361.1 15.4 %fusion.5 = f32[128,2048]{0,1:T(8,128)} fusion(bf16[3,8,16,8,2048]{4,2,3,1,0:T(8,128)(2,1)} %all-gather.2.cloned.1.call-done, f32[3,8,16,8,128]{4,3,2,1,0:T(8,128)} %bitcast.45), kind=kOutput, calls=%fused_computation.6 | convolution fusion | flops 1611268096 | bytes 15204352 | tf_op jit(solution)/shard_map/ra,rk->ak/dot_general | solution.py:81
  376.6 0.0 reduce-scatter.2.cloned.1.call-update
  376.6 0.7 copy.44
  377.3 0.0 copy-done.3
  377.3 1.7 copy.43
  379.1 105.6 %reduce-scatter.2.cloned.1.call-done = f32[128,64]{0,1:T(8,128)} async-done(((f32[128,2048]{0,1:T(8,128)}), f32[128,64]{0,1:T(8,128)}) %reduce-scatter.2.cloned.1.call-update) | async-done | bytes 32784 | tf_op jit(solution)/shard_map/reduce_scatter | solution.py:84
  (2 shorter events, 0.1 us)
Async XLA Ops:
  7.2 1.4 copy-start
  7.2 4.7 copy-start.5
  7.2 4.8 copy-start.6
  7.2 192.2 %all-reduce.4.cloned.1.call-start = ((), (), s32[]{:S(2)}) async-start(), calls=%async_computation.1 | async-start | bytes 131072 | tf_op jit(solution)/shard_map/psum | solution.py:71
  11.9 349.3 %all-gather.2.cloned.1.call-start = ((), (), s32[]{:S(2)}) async-start(), calls=%async_computation.2 | async-start | bytes 13369344 | tf_op jit(solution)/shard_map/all_gather | solution.py:78
  230.3 7.0 %copy-start.1 = (f32[3,8,16,8,128]{4,2,3,1,0:T(8,128)}, f32[3,8,16,8,128]{4,2,3,1,0:T(8,128)S(1)}, u32[]{:S(2)}) copy-start(f32[3,8,16,8,128]{4,2,3,1,0:T(8,128)S(1)} %copy.30) | copy-start | bytes 4718596
  231.1 14.7 %collective-permute-start = (f32[3,1,16,8,128]{4,2,3,1,0:T(8,128)}, f32[3,1,16,8,128]{4,2,3,1,0:T(8,128)}, u32[]{:S(2)}, u32[]{:S(2)}) collective-permute-start(f32[3,1,16,8,128]{4,2,3,1,0:T(8,128)} %get-tuple-element.11), channel_id=1, source_target_pairs={{16,0},{32,16},{48,32},{64,48},{80,64},{96,80},{112,96},{128,112},... | collective-permute-start | bytes 589832 | tf_op jit(solution)/shard_map/ppermute | solution.py:17
  232.4 13.4 %collective-permute-start.1 = (f32[3,1,16,8,128]{4,2,3,1,0:T(8,128)}, f32[3,1,16,8,128]{4,2,3,1,0:T(8,128)}, u32[]{:S(2)}, u32[]{:S(2)}) collective-permute-start(f32[3,1,16,8,128]{4,2,3,1,0:T(8,128)} %get-tuple-element.12), channel_id=1, source_target_pairs={{0,16},{16,32},{32,48},{48,64},{64,80},{80,96},{96,112},{112,128},... | collective-permute-start | bytes 589832 | tf_op jit(solution)/shard_map/ppermute | solution.py:15
  237.3 2.2 copy-start.4
  240.5 5.3 %copy-start.2 = (f32[3,8,16,8,128]{4,2,3,1,0:T(8,128)S(1)}, f32[3,8,16,8,128]{4,2,3,1,0:T(8,128)}, u32[]{:S(2)}) copy-start(f32[3,8,16,8,128]{4,2,3,1,0:T(8,128)} %copy-done.1) | copy-start | bytes 4718596
  250.8 233.9 %reduce-scatter.2.cloned.1.call-start = ((), (), s32[]{:S(2)}) async-start(), calls=%async_computation.3 | async-start | bytes 1081344 | tf_op jit(solution)/shard_map/reduce_scatter | solution.py:84
  361.1 16.2 %copy-start.3 = (f32[3,8,16,8,128]{4,2,3,1,0:T(8,128)S(1)}, f32[3,8,16,8,128]{4,2,3,1,0:T(8,128)}, u32[]{:S(2)}) copy-start(f32[3,8,16,8,128]{4,2,3,1,0:T(8,128)} %get-tuple-element.10) | copy-start | bytes 4718596
Sparse Core Ops, SparseCore 0:
  12.0 187.3 all-reduce.3
  250.9 110.1 all-gather.1
  376.7 107.9 reduce-scatter.1
where the time goes:
time: 492 us; the launch traced here: 491 us
  waiting for transfers between devices  403 us (82%)
  other arithmetic  29.3 us (6%)
  matrix products  21 us (4%)
  local copies, waits for them, and re-layouts  19.2 us (4%)
  between operations  13.9 us (3%)
  starting transfers between devices  5.11 us (1%)
    psum x1, waiting for transfers between devices, body(): gram = lax.psum(gram_local, 'space')  187 us
    all_gather x1, waiting for transfers between devices, body(): panel_piece = lax.all_gather(rounded_images, 'mode', axis=4, tiled=True)  110 us
    reduce_scatter x1, waiting for transfers between devices, body(): reduced = lax.psum_scatter(strip, 'space', scatter_dimension=1, tiled=True)  106 us
    dot_general x1, matrix products, body(): jnp.einsum('ra,rk->ak', rounded_rows, piece_rows, preferred_element_type=...  15.4 us
    another operation x3, other arithmetic, body(): lower_factor = jnp.linalg.cholesky(gram)  12.4 us
    another operation x1, other arithmetic, apply_inverse(): jax.scipy.linalg.solve_triangular(lower_factor, flat_rows.T, lower=True)  10.4 us
  transfers between devices with their start and end apart: 5, of which 3 were waited for; matrix products, arithmetic and copies ran while one was open for 3% of the time, Pallas kernels for 0%

commit v1 on v0

--- a/solution.py
+++ b/solution.py
@@ -53,6 +53,11 @@
 
 
 def body(basis, mean_flow, flow_gradient, viscosity):
+
+    def cover_tokens(vector, dev_axis):
+        clean = lax.all_gather(vector, dev_axis)
+        return jnp.sum(clean, axis=0)
+
     cells_x = basis.shape[1]
     cells_y = basis.shape[2]
     cells_z = basis.shape[3]
@@ -68,7 +73,7 @@
         )
         * weight
     )
-    gram = lax.psum(gram_local, "space")
+    gram = cover_tokens(gram_local, "space")
     lower_factor = jnp.linalg.cholesky(gram)
     ortho = apply_inverse(basis, lower_factor)
     padded_ortho = extended(ortho, (("space", 1),), 1)

time: 492 us -> 374 us (0.76)
  waiting for transfers between devices: 403 us -> 292 us
  matrix products: 21 us -> 15 us
    psum x1 -> x0, waiting for transfers between devices: 187 us -> none  [body(): gram = lax.psum(gram_local, 'space')]
    all_gather x0 -> x1, waiting for transfers between devices: none -> 72.4 us  [cover_tokens(): clean = lax.all_gather(vector, dev_axis)]
    dot_general x1, matrix products: 15.4 us -> 9.03 us  [body(): jnp.einsum('ra,rk->ak', rounded_rows, piece_rows, preferred_element_type=...]
  transfers between devices with their start and end apart: 5 -> 5, of which waited for: 3 -> 3; matrix products, arithmetic and copies ran while one was open for 3% -> 4% of each run, Pallas kernels for 0% -> 0%
where the time goes in v1:
time: 374 us
  waiting for transfers between devices  292 us (78%)
  other arithmetic  30.3 us (8%)
  local copies, waits for them, and re-layouts  17.4 us (5%)
  matrix products  15 us (4%)
  between operations  13.9 us (4%)
  starting transfers between devices  5.12 us (1%)
    all_gather x1, waiting for transfers between devices, body(): panel_piece = lax.all_gather(rounded_images, 'mode', axis=4, tiled=True)  112 us
    reduce_scatter x1, waiting for transfers between devices, body(): reduced = lax.psum_scatter(strip, 'space', scatter_dimension=1, tiled=True)  107 us
    all_gather x1, waiting for transfers between devices, cover_tokens(): clean = lax.all_gather(vector, dev_axis)  72.4 us
    another operation x3, other arithmetic, body(): lower_factor = jnp.linalg.cholesky(gram)  12.4 us
    another operation x1, other arithmetic, apply_inverse(): jax.scipy.linalg.solve_triangular(lower_factor, flat_rows.T, lower=True)  9.81 us
    dot_general x1, matrix products, body(): jnp.einsum('ra,rk->ak', rounded_rows, piece_rows, preferred_element_type=...  9.03 us
  transfers between devices with their start and end apart: 5, of which 3 were waited for; matrix products, arithmetic and copies ran while one was open for 4% of the time, Pallas kernels for 0%

profile of v1, /device:TPU:2, one launch (start us, length us, event | category | flops | bytes accessed | tf_op | source)
XLA Modules:
  0.0 373.8 jit_solution(15317544143609956054)
XLA Ops:
  7.2 0.0 copy-start
  7.2 0.0 copy-start.4
  7.2 0.0 copy-start.3
  7.2 0.0 copy-start.1
  7.2 0.0 all-gather.6.cloned.1.call-start
  7.3 1.3 copy-done
  8.6 3.3 fusion.1
  11.8 0.0 all-gather.6.cloned.1.call-update
  11.9 0.0 all-gather.4.cloned.1.call-start
  11.9 0.0 copy-done.4
  11.9 0.7 copy.45
  12.7 0.0 copy-done.3
  12.7 0.7 copy.46
  13.4 0.7 copy.48
  14.1 0.7 copy.47
  14.8 0.0 copy-done.1
  14.8 0.1 copy.49
  14.9 0.1 copy.53
  15.0 0.8 copy.51
  15.8 72.4 %all-gather.6.cloned.1.call-done = f32[4096,128]{1,0:T(8,128)} async-done(((f32[128,128]{1,0:T(8,128)}), f32[4096,128]{1,0:T(8,128)}) %all-gather.6.cloned.1.call-update) | async-done | bytes 2097168 | tf_op jit(solution)/shard_map/all_gather | solution.py:58
  88.3 1.7 reduce_sum.9
  90.0 0.1 copy.43
  90.1 11.7 %cholesky.16 = f32[128,128]{1,0:T(8,128)S(1)} custom-call(f32[128,128]{1,0:T(8,128)S(1)} %fusion.4), custom_call_target="Cholesky" | custom-call | tf_op jit(solution)/shard_map/jit(cholesky)/cholesky | solution.py:77
  101.9 0.6 compare_reduce_fusion
  102.5 1.3 fusion.5
  103.8 9.8 %custom-call.7 = f32[1,128,128]{1,2,0:T(8,128)S(1)} custom-call(f32[1,128,128]{2,1,0:T(8,128)S(1)} %get-tuple-element.26), custom_call_target="InvertDiagBlocksLowerTriangular" | custom-call | tf_op jit(solution)/shard_map/jit(_solve_triangular)/triangular_solve | solution.py:51
  113.6 2.7 convolution_bitcast_fusion
  116.3 1.9 copy.44
  118.1 0.8 fusion.7
  118.9 1.3 collective-permute-start
  120.2 3.7 collective-permute-start.1
  123.9 2.6 fusion.8
  126.5 2.0 copy.50
  128.5 2.0 copy.54
  130.5 2.1 copy.52
  132.6 0.0 collective-permute-done
  132.6 0.0 collective-permute-done.1
  132.6 5.1 %fusion.6 = (bf16[3,8,16,8,128]{4,3,2,1,0:T(8,128)(2,1)}, f32[3,8,16,8,128]{4,3,2,1,0:T(8,128)}) fusion(f32[8,16,8,128]{3,2,1,0:T(8,128)} %bitcast.52, f32[3,8,16,8]{3,2,1,0:T(8,128)S(1)} %copy.53, f32[8,16,8,128]{3,2,1,0:T(8,128)} %bitcast.53, f32[3,8,16,8]{3,2,1,0:T(8,128)} %copy.51, f32[8,16,8,128]{3,2,1,0:T(8,128)} %bitcast.51, ...), kind=kLoop, calls=%fused_computation.29 | loop fusion | flops 10616832 | bytes 5951488 | tf_op jit(solution)/shard_map/convert_element_type | solution.py:81
  137.7 0.0 all-gather.4.cloned.1.call-update
  137.8 0.0 copy-start.2
  137.8 0.0 reduce-scatter.2.cloned.1.call-start
  137.8 112.3 %all-gather.4.cloned.1.call-done = bf16[3,8,16,8,2048]{4,3,2,1,0:T(8,128)(2,1)} async-done(((bf16[3,8,16,8,128]{4,3,2,1,0:T(8,128)(2,1)}), bf16[3,8,16,8,2048]{4,3,2,1,0:T(8,128)(2,1)}) %all-gather.4.cloned.1.call-update) | async-done | bytes 12582928 | tf_op jit(solution)/shard_map/all_gather | solution.py:83
  250.2 9.0 %fusion = f32[128,2048]{0,1:T(8,128)} fusion(bf16[3,8,16,8,2048]{4,3,2,1,0:T(8,128)(2,1)} %all-gather.4.cloned.1.call-done, f32[3,8,16,8,128]{4,3,2,1,0:T(8,128)S(1)} %bitcast.50), kind=kOutput, calls=%fused_computation.4 | convolution fusion | flops 1611268096 | bytes 15204352 | tf_op jit(solution)/shard_map/ra,rk->ak/dot_general | solution.py:86
  259.2 0.0 reduce-scatter.2.cloned.1.call-update
  259.2 0.0 copy-done.2
  259.2 0.7 copy.55
  260.0 107.3 %reduce-scatter.2.cloned.1.call-done = f32[128,64]{0,1:T(8,128)} async-done(((f32[128,2048]{0,1:T(8,128)}), f32[128,64]{0,1:T(8,128)}) %reduce-scatter.2.cloned.1.call-update) | async-done | bytes 32784 | tf_op jit(solution)/shard_map/reduce_scatter | solution.py:89
  (4 shorter events, 0.1 us)
Async XLA Ops:
  7.2 1.4 copy-start
  7.2 4.7 %copy-start.4 = (f32[8,16,8]{1,2,0:T(8,128)S(1)}, f32[8,16,8]{1,2,0:T(8,128)}, u32[]{:S(2)}) copy-start(f32[8,16,8]{1,2,0:T(8,128)} %param.7) | copy-start | bytes 12292
  7.2 5.5 %copy-start.3 = (f32[3,8,16,8]{2,3,1,0:T(8,128)S(1)}, f32[3,8,16,8]{2,3,1,0:T(8,128)}, u32[]{:S(2)}) copy-start(f32[3,8,16,8]{2,3,1,0:T(8,128)} %param.5) | copy-start | bytes 36868
  7.2 7.6 %copy-start.1 = (f32[3,3,8,16,8]{3,4,2,1,0:T(8,128)S(1)}, f32[3,3,8,16,8]{3,4,2,1,0:T(8,128)}, u32[]{:S(2)}) copy-start(f32[3,3,8,16,8]{3,4,2,1,0:T(8,128)} %param.6) | copy-start | bytes 110596
  7.2 81.1 %all-gather.6.cloned.1.call-start = ((), (), s32[]{:S(2)}) async-start(), calls=%async_computation.3 | async-start | bytes 2162688 | tf_op jit(solution)/shard_map/all_gather | solution.py:58
  11.9 238.3 %all-gather.4.cloned.1.call-start = ((), (), s32[]{:S(2)}) async-start(), calls=%async_computation.1 | async-start | bytes 13369344 | tf_op jit(solution)/shard_map/all_gather | solution.py:83
  118.9 13.7 %collective-permute-start = (f32[3,1,16,8,128]{4,3,2,1,0:T(8,128)}, f32[3,1,16,8,128]{4,3,2,1,0:T(8,128)}, u32[]{:S(2)}, u32[]{:S(2)}) collective-permute-start(f32[3,1,16,8,128]{4,3,2,1,0:T(8,128)} %get-tuple-element.14), channel_id=1, source_target_pairs={{16,0},{32,16},{48,32},{64,48},{80,64},{96,80},{112,96},{128,112},... | collective-permute-start | bytes 589832 | tf_op jit(solution)/shard_map/ppermute | solution.py:17
  120.2 12.4 %collective-permute-start.1 = (f32[3,1,16,8,128]{4,3,2,1,0:T(8,128)}, f32[3,1,16,8,128]{4,3,2,1,0:T(8,128)}, u32[]{:S(2)}, u32[]{:S(2)}) collective-permute-start(f32[3,1,16,8,128]{4,3,2,1,0:T(8,128)} %get-tuple-element.15), channel_id=1, source_target_pairs={{0,16},{16,32},{32,48},{48,64},{64,80},{80,96},{96,112},{112,128},... | collective-permute-start | bytes 589832 | tf_op jit(solution)/shard_map/ppermute | solution.py:15
  137.8 121.5 %copy-start.2 = (f32[128,128]{0,1:T(8,128)S(1)}, f32[128,128]{0,1:T(8,128)}, u32[]{:S(2)}) copy-start(f32[128,128]{0,1:T(8,128)} %get-tuple-element.25) | copy-start | bytes 196612
  137.8 229.5 %reduce-scatter.2.cloned.1.call-start = ((), (), s32[]{:S(2)}) async-start(), calls=%async_computation.2 | async-start | bytes 1081344 | tf_op jit(solution)/shard_map/reduce_scatter | solution.py:89
Sparse Core Ops, SparseCore 0:
  12.0 76.2 all-gather.5
  137.9 112.2 all-gather.3
  259.3 107.9 reduce-scatter.1
